TPU v7x, 32 devices: a whole 2x2x4 slice. The times are simulated.
32 devices in a mesh: ctx: 16 (over z, y, core), exp: 2 (over x).
Axes of the slice: x: 2, y: 2, z: 4, core: 2. Of those that a mesh axis runs over, the one named last changes fastest.
Arguments:
- queries: bfloat16 [2, 2048, 2048], P('exp', 'ctx'), may hold values from -64 to 64
- rotated_key_rows: bfloat16 [2, 2048, 256], P('exp', 'ctx'), may hold values from -7 to 7
- value_row_array: bfloat16 [2, 2048, 256], P('exp', 'ctx'), may hold values from -6 to 6
- residual: bfloat16 [2, 2048, 2048], P('exp', 'ctx'), may hold values from -40 to 40
- norm_gain: float32 [2048], replicated, may hold values from 0.1 to 1.9
- expert_ids: int32 [2, 2048, 1], P('exp', 'ctx'), may hold values from 0 to 7; in each aligned block of 128 rows (0 to 127, 128 to 255, ..., all dimensions but the last counted through in order) at most 32 rows name the same one
- gate_values: float32 [2, 2048, 1], P('exp', 'ctx'), may hold values from 0.25 to 1
- w_gate_up: bfloat16 [16, 2, 2, 192, 2048], P('ctx', 'exp'), may hold values from -0.125 to 0.125
- w_down: bfloat16 [16, 2, 192, 2048], P('ctx', 'exp'), may hold values from -0.21875 to 0.21875
Outputs:
- layer_out: bfloat16 [2, 2048, 2048], P('exp', 'ctx')
Inputs may be any that keep to these rules, and one draw needn't show every extreme that they name: `expert_ids`: among the rows of one device (aligned blocks of 128 tokens along the second dimension) no expert is named more than 32 times, a bound that some block reaches.
All inputs are finite; a program needn't handle non-finite values.
Results may differ from a plain program's by a relative error of at most 0.013.
Values may be sent and summed in bfloat16 or wider, within the bound.
A program may use at most 64 MiB of HBM per device.

v0:
```python
import math

import jax
import jax.numpy as jnp
from jax import lax
from jax.sharding import PartitionSpec as P

D = 2048
QUERY_HEADS = 16
KEY_VALUE_HEADS = 2
HEAD_SIZE = 128
TOP = 1


NEGATIVE_FILL = -1e30


def passed_along(value, axis, steps):
    count = lax.axis_size(axis)
    leading, last = (max(0, -steps), min(count, count - steps))
    return lax.ppermute(value, axis, [(source, source + steps) for source in range(leading, last)])


def attend_piece(soft_state, query_head_rows, key_value_block, allowed):
    row_peak, row_total, weighted_sum = soft_state
    block_key_rows = key_value_block[0].reshape(-1, KEY_VALUE_HEADS, HEAD_SIZE)
    block_value_rows = key_value_block[1].reshape(-1, KEY_VALUE_HEADS, HEAD_SIZE)
    scores = jnp.einsum(
        "qhgd,khd->hgqk", query_head_rows, block_key_rows, preferred_element_type=jnp.float32
    ) / math.sqrt(HEAD_SIZE)
    if allowed is not None:
        scores = jnp.where(allowed, scores, NEGATIVE_FILL)
    new_peak = jnp.maximum(row_peak, jnp.max(scores, axis=-1))
    expo_vals = jnp.exp(scores - new_peak[..., None])
    factor = jnp.exp(row_peak - new_peak)
    row_total = row_total * factor + jnp.sum(expo_vals, axis=-1)
    weights = expo_vals.astype(jnp.bfloat16)
    weighted_sum = weighted_sum * factor[..., None] + jnp.einsum(
        "hgqk,khd->hgqd", weights, block_value_rows, preferred_element_type=jnp.float32
    )
    return (new_peak, row_total, weighted_sum)


def on_device(
    queries,
    rotated_key_rows,
    value_row_array,
    residual,
    norm_gain,
    expert_ids,
    gate_values,
    w_gate_up,
    w_down,
):
    ctx_count = lax.axis_size("ctx")
    exp_count = lax.axis_size("exp")
    token_rows = queries.shape[1]
    queries_per_key_head = QUERY_HEADS // KEY_VALUE_HEADS
    query_head_rows = queries[0].reshape(
        token_rows, KEY_VALUE_HEADS, queries_per_key_head, HEAD_SIZE
    )
    prompt_devs = ctx_count // 2
    ctx_index = lax.axis_index("ctx")
    in_prompt = ctx_index // 2
    own_block = jnp.stack([rotated_key_rows[0], value_row_array[0]])
    diagonal = jnp.arange(token_rows)[:, None] >= jnp.arange(token_rows)[None, :]
    start_state = (
        jnp.full((KEY_VALUE_HEADS, queries_per_key_head, token_rows), NEGATIVE_FILL, jnp.float32),
        jnp.zeros((KEY_VALUE_HEADS, queries_per_key_head, token_rows), jnp.float32),
        jnp.zeros((KEY_VALUE_HEADS, queries_per_key_head, token_rows, HEAD_SIZE), jnp.float32),
    )
    soft_state = attend_piece(start_state, query_head_rows, own_block, diagonal)

    def carry_step(step_index, carried):
        current_state, moving = carried
        moving = passed_along(moving, "ctx", 2)
        current_state = lax.cond(
            step_index <= in_prompt,
            lambda state_in: attend_piece(state_in, query_head_rows, moving, None),
            lambda state_in: state_in,
            current_state,
        )
        return (current_state, moving)

    soft_state, _ = lax.fori_loop(1, prompt_devs, carry_step, (soft_state, own_block))
    row_peak, row_total, weighted_sum = soft_state
    attended_rows = weighted_sum / row_total[..., None]
    attended_rows = jnp.transpose(attended_rows, (2, 0, 1, 3)).reshape(
        token_rows, QUERY_HEADS * HEAD_SIZE
    )
    mid_rows = (residual[0].astype(jnp.float32) + attended_rows).astype(jnp.bfloat16)
    mid_wide = mid_rows.astype(jnp.float32)
    inverse = lax.rsqrt(jnp.mean(mid_wide * mid_wide, axis=-1, keepdims=True) + 1e-06)
    normed = (mid_wide * inverse * norm_gain).astype(jnp.bfloat16)
    per_group = ctx_count // 4
    expert_count = per_group * exp_count
    slot_depth = max(2, 2 * token_rows * TOP // expert_count)
    assign_count = token_rows * TOP
    routed = expert_ids[0].reshape(assign_count)
    onehot_table = (routed[:, None] == jnp.arange(expert_count)[None, :]).astype(jnp.float32)
    earlier_blocks = (jnp.arange(assign_count)[:, None] > jnp.arange(assign_count)[None, :]).astype(
        jnp.float32
    )
    before = jnp.dot(
        earlier_blocks,
        onehot_table,
        precision=lax.Precision.HIGHEST,
        preferred_element_type=jnp.float32,
    )
    rank_in = jnp.sum(before * onehot_table, axis=1).astype(jnp.int32)
    slot_index = (routed % per_group * exp_count + routed // per_group) * slot_depth + rank_in
    slot_count = expert_count * slot_depth
    placement = (jnp.arange(slot_count)[:, None] == slot_index[None, :]).astype(jnp.bfloat16)
    normed_assign = jnp.repeat(normed, TOP, axis=0)
    outgoing = jnp.dot(placement, normed_assign, preferred_element_type=jnp.float32).astype(
        jnp.bfloat16
    )
    outgoing = outgoing.reshape(per_group, exp_count, slot_depth, D)
    incoming = lax.all_to_all(outgoing, "exp", split_axis=1, concat_axis=1, tiled=True)
    slot_width = exp_count * slot_depth
    by_expert = incoming.reshape(per_group, slot_width, D)
    gate_up = w_gate_up[0, 0]
    down_rows = w_down[0, 0]
    copies = jnp.broadcast_to(by_expert[:, None], (per_group, 4, slot_width, D)).reshape(
        ctx_count, slot_width, D
    )
    arrived = lax.all_to_all(copies, "ctx", split_axis=0, concat_axis=0, tiled=True)
    lead_shape = arrived.shape[:-1]
    flat_rows = arrived.reshape(-1, D)
    projected = lax.dot_general(
        gate_up, flat_rows, (((2,), (1,)), ((), ())), preferred_element_type=jnp.float32
    )
    hidden = (jax.nn.silu(projected[0]) * projected[1]).astype(jnp.bfloat16)
    part_out = lax.dot_general(
        hidden, down_rows, (((0,), (0,)), ((), ())), preferred_element_type=jnp.float32
    )
    partial_value = part_out.astype(jnp.bfloat16).reshape(lead_shape + (D,))
    returned = lax.all_to_all(partial_value, "ctx", split_axis=0, concat_axis=0, tiled=True)
    returned = returned.reshape(per_group, 4, slot_width, D)
    summed = (
        returned[:, 0].astype(jnp.float32)
        + returned[:, 1].astype(jnp.float32)
        + returned[:, 2].astype(jnp.float32)
        + returned[:, 3].astype(jnp.float32)
    ).astype(jnp.bfloat16)
    delivered = lax.all_to_all(
        summed.reshape(per_group, exp_count, slot_depth, D),
        "exp",
        split_axis=1,
        concat_axis=1,
        tiled=True,
    )
    expert_out = lax.dot_general(
        placement,
        delivered.reshape(slot_count, D),
        (((0,), (0,)), ((), ())),
        preferred_element_type=jnp.float32,
    )
    gated = expert_out.reshape(token_rows, TOP, D) * gate_values[0][:, :, None]
    layer_out = (mid_wide + jnp.sum(gated, axis=1)).astype(jnp.bfloat16)
    return layer_out[None]


def solution(mesh):
    return jax.shard_map(
        on_device,
        mesh=mesh,
        in_specs=(
            P("exp", "ctx", None),
            P("exp", "ctx", None),
            P("exp", "ctx", None),
            P("exp", "ctx", None),
            P(),
            P("exp", "ctx", None),
            P("exp", "ctx", None),
            P("ctx", "exp", None, None, None),
            P("ctx", "exp", None, None),
        ),
        out_specs=P("exp", "ctx", None),
        check_vma=False,
    )
```

profile of v0, /device:TPU:0, one launch (start us, length us, event | category | flops | bytes accessed | tf_op | source)
XLA Modules:
  0.0 313.1 jit_solution(10438892226590195380)
XLA Ops:
  0.0 1.1 copy.72
  4.7 1.2 convert_add_fusion.1
  5.9 1.3 copy.67
  9.1 1.2 copy.98
  10.3 1.7 convolution_add_fusion.1
  12.0 56.7 %while.19 = (s32[]{:T(128)}, f32[2,8,128]{2,1,0:T(8,128)S(1)}, f32[2,8,128]{2,1,0:T(8,128)S(1)}, f32[2,8,128,128]{3,2,1,0:T(8,128)S(1)}, bf16[2,128,256]{1,2,0:T...) while((s32[]{:T(128)}, f32[2,8,128]{2,1,0:T(8,128)S(1)}, ...), condition=%wide.region_7.8_spmd, body=%wide.region_2.7_spmd.sunk | while | flops 136318976 | bytes 7078123 | solution.py:85
  12.0 4.9 %collective-permute-start = (bf16[2,128,256]{1,2,0:T(8,128)(2,1)S(1)}, bf16[2,128,256]{1,2,0:T(8,128)(2,1)S(1)}, u32[]{:S(2)}, u32[]{:S(2)}) collective-permute-start(bf16[2,128,256]{1,2,0:T(8,128)(2,1)S(1)} %get-tuple-element.283), channel_id=1, source_target_pairs={{0,4},{2,6},{4,8},{6,10},{8,12},{10,14},{12,16},{14,18},{16,20},{1... | collective-permute-start | bytes 393224 | tf_op jit(solution)/shard_map/while/body/eval_jaxpr/ppermute | solution.py:21
  16.9 2.7 collective-permute-done
  19.7 5.7 %collective-permute-start = (bf16[2,128,256]{1,2,0:T(8,128)(2,1)S(1)}, bf16[2,128,256]{1,2,0:T(8,128)(2,1)S(1)}, u32[]{:S(2)}, u32[]{:S(2)}) collective-permute-start(bf16[2,128,256]{1,2,0:T(8,128)(2,1)S(1)} %get-tuple-element.283), channel_id=1, source_target_pairs={{0,4},{2,6},{4,8},{6,10},{8,12},{10,14},{12,16},{14,18},{16,20},{1... | collective-permute-start | bytes 393224 | tf_op jit(solution)/shard_map/while/body/eval_jaxpr/ppermute | solution.py:21
  25.4 2.5 collective-permute-done
  27.9 4.4 %collective-permute-start = (bf16[2,128,256]{1,2,0:T(8,128)(2,1)S(1)}, bf16[2,128,256]{1,2,0:T(8,128)(2,1)S(1)}, u32[]{:S(2)}, u32[]{:S(2)}) collective-permute-start(bf16[2,128,256]{1,2,0:T(8,128)(2,1)S(1)} %get-tuple-element.283), channel_id=1, source_target_pairs={{0,4},{2,6},{4,8},{6,10},{8,12},{10,14},{12,16},{14,18},{16,20},{1... | collective-permute-start | bytes 393224 | tf_op jit(solution)/shard_map/while/body/eval_jaxpr/ppermute | solution.py:21
  32.2 2.5 collective-permute-done
  34.8 6.5 %collective-permute-start = (bf16[2,128,256]{1,2,0:T(8,128)(2,1)S(1)}, bf16[2,128,256]{1,2,0:T(8,128)(2,1)S(1)}, u32[]{:S(2)}, u32[]{:S(2)}) collective-permute-start(bf16[2,128,256]{1,2,0:T(8,128)(2,1)S(1)} %get-tuple-element.283), channel_id=1, source_target_pairs={{0,4},{2,6},{4,8},{6,10},{8,12},{10,14},{12,16},{14,18},{16,20},{1... | collective-permute-start | bytes 393224 | tf_op jit(solution)/shard_map/while/body/eval_jaxpr/ppermute | solution.py:21
  41.3 2.5 collective-permute-done
  43.8 5.3 %collective-permute-start = (bf16[2,128,256]{1,2,0:T(8,128)(2,1)S(1)}, bf16[2,128,256]{1,2,0:T(8,128)(2,1)S(1)}, u32[]{:S(2)}, u32[]{:S(2)}) collective-permute-start(bf16[2,128,256]{1,2,0:T(8,128)(2,1)S(1)} %get-tuple-element.283), channel_id=1, source_target_pairs={{0,4},{2,6},{4,8},{6,10},{8,12},{10,14},{12,16},{14,18},{16,20},{1... | collective-permute-start | bytes 393224 | tf_op jit(solution)/shard_map/while/body/eval_jaxpr/ppermute | solution.py:21
  49.1 2.5 collective-permute-done
  51.6 5.4 %collective-permute-start = (bf16[2,128,256]{1,2,0:T(8,128)(2,1)S(1)}, bf16[2,128,256]{1,2,0:T(8,128)(2,1)S(1)}, u32[]{:S(2)}, u32[]{:S(2)}) collective-permute-start(bf16[2,128,256]{1,2,0:T(8,128)(2,1)S(1)} %get-tuple-element.283), channel_id=1, source_target_pairs={{0,4},{2,6},{4,8},{6,10},{8,12},{10,14},{12,16},{14,18},{16,20},{1... | collective-permute-start | bytes 393224 | tf_op jit(solution)/shard_map/while/body/eval_jaxpr/ppermute | solution.py:21
  57.0 3.5 %collective-permute-done = bf16[2,128,256]{1,2,0:T(8,128)(2,1)S(1)} collective-permute-done((bf16[2,128,256]{1,2,0:T(8,128)(2,1)S(1)}, bf16[2,128,256]{1,2,0:T(8,128)(2,1)S(1)}, u32[]{:S(2)}, u32[]{:S(2)}) %collective-permute-start) | collective-permute-done | bytes 131104 | tf_op jit(solution)/shard_map/while/body/eval_jaxpr/ppermute | solution.py:21
  60.6 5.6 %collective-permute-start = (bf16[2,128,256]{1,2,0:T(8,128)(2,1)S(1)}, bf16[2,128,256]{1,2,0:T(8,128)(2,1)S(1)}, u32[]{:S(2)}, u32[]{:S(2)}) collective-permute-start(bf16[2,128,256]{1,2,0:T(8,128)(2,1)S(1)} %get-tuple-element.283), channel_id=1, source_target_pairs={{0,4},{2,6},{4,8},{6,10},{8,12},{10,14},{12,16},{14,18},{16,20},{1... | collective-permute-start | bytes 393224 | tf_op jit(solution)/shard_map/while/body/eval_jaxpr/ppermute | solution.py:21
  66.2 2.5 collective-permute-done
  68.7 1.9 multiply_reduce_fusion
  72.0 11.9 %all_to_all.20 = bf16[4,2,32,2048]{3,2,0,1:T(8,128)(2,1)S(1)} all-to-all(bf16[4,2,32,2048]{3,2,0,1:T(8,128)(2,1)S(1)} %copy.78), channel_id=1, replica_groups=mesh['ctx'=16,'exp'=2] {'exp'}, dimensions={1} | all-to-all | bytes 2097152 | tf_op jit(solution)/shard_map/all_to_all | solution.py:119
  84.5 104.4 %all_to_all.21 = bf16[16,64,2048]{2,1,0:T(8,128)(2,1)S(1)} all-to-all(bf16[16,64,2048]{2,1,0:T(8,128)(2,1)S(1)} %bitcast.83), channel_id=1, replica_groups=mesh['ctx'=16,'exp'=2] {'ctx'}, dimensions={0} | all-to-all | bytes 8388608 | tf_op jit(solution)/shard_map/all_to_all | solution.py:127
  188.9 1.9 fusion.10
  190.8 1.3 convolution_convert_fusion
  192.1 97.4 %all_to_all.22 = bf16[16,64,2048]{2,1,0:T(8,128)(2,1)S(1)} all-to-all(bf16[16,64,2048]{2,1,0:T(8,128)(2,1)S(1)} %bitcast.94), channel_id=1, replica_groups=mesh['ctx'=16,'exp'=2] {'ctx'}, dimensions={0} | all-to-all | bytes 8388608 | tf_op jit(solution)/shard_map/all_to_all | solution.py:138
  290.2 1.1 copy.80
  291.3 4.4 %all-to-all-start.3 = ((bf16[4,2,32,2048]{3,2,0,1:T(8,128)(2,1)}), bf16[4,2,32,2048]{3,2,0,1:T(8,128)(2,1)}, u32[]{:S(2)}, u32[]{:S(2)}) async-start(bf16[4,2,32,2048]{3,2,0,1:T(8,128)(2,1)} %copy.80), calls=%async_computation.3 | async-start | bytes 2097152 | tf_op jit(solution)/shard_map/all_to_all | solution.py:146
  295.7 1.1 reshape.127
  296.9 13.7 %all-to-all-done.3 = bf16[4,2,32,2048]{3,2,0,1:T(8,128)(2,1)} async-done(((bf16[4,2,32,2048]{3,2,0,1:T(8,128)(2,1)}), bf16[4,2,32,2048]{3,2,0,1:T(8,128)(2,1)}, u32[]{:S(2)}, u32[]{:S(2)}) %all-to-all-start.3) | async-done | bytes 1048608 | tf_op jit(solution)/shard_map/all_to_all | solution.py:146
  310.6 1.3 copy.81
  311.9 1.2 fusion.7
  (53 shorter events, 8.3 us)
Async XLA Ops:
  0.0 188.9 %copy-start = (bf16[1,1,2,192,2048]{4,3,2,1,0:T(8,128)(2,1)S(1)}, bf16[1,1,2,192,2048]{4,3,2,1,0:T(8,128)(2,1)}, u32[]{:S(2)}) copy-start(bf16[1,1,2,192,2048]{4,3,2,1,0:T(8,128)(2,1)} %param.20) | copy-start | bytes 4718596
  7.2 1.8 copy-start.2
  7.8 1.0 copy-start.1
  12.0 7.6 %collective-permute-start = (bf16[2,128,256]{1,2,0:T(8,128)(2,1)S(1)}, bf16[2,128,256]{1,2,0:T(8,128)(2,1)S(1)}, u32[]{:S(2)}, u32[]{:S(2)}) collective-permute-start(bf16[2,128,256]{1,2,0:T(8,128)(2,1)S(1)} %get-tuple-element.283), channel_id=1, source_target_pairs={{0,4},{2,6},{4,8},{6,10},{8,12},{10,14},{12,16},{14,18},{16,20},{1... | collective-permute-start | bytes 393224 | tf_op jit(solution)/shard_map/while/body/eval_jaxpr/ppermute | solution.py:21
  19.7 8.2 %collective-permute-start = (bf16[2,128,256]{1,2,0:T(8,128)(2,1)S(1)}, bf16[2,128,256]{1,2,0:T(8,128)(2,1)S(1)}, u32[]{:S(2)}, u32[]{:S(2)}) collective-permute-start(bf16[2,128,256]{1,2,0:T(8,128)(2,1)S(1)} %get-tuple-element.283), channel_id=1, source_target_pairs={{0,4},{2,6},{4,8},{6,10},{8,12},{10,14},{12,16},{14,18},{16,20},{1... | collective-permute-start | bytes 393224 | tf_op jit(solution)/shard_map/while/body/eval_jaxpr/ppermute | solution.py:21
  27.9 6.9 %collective-permute-start = (bf16[2,128,256]{1,2,0:T(8,128)(2,1)S(1)}, bf16[2,128,256]{1,2,0:T(8,128)(2,1)S(1)}, u32[]{:S(2)}, u32[]{:S(2)}) collective-permute-start(bf16[2,128,256]{1,2,0:T(8,128)(2,1)S(1)} %get-tuple-element.283), channel_id=1, source_target_pairs={{0,4},{2,6},{4,8},{6,10},{8,12},{10,14},{12,16},{14,18},{16,20},{1... | collective-permute-start | bytes 393224 | tf_op jit(solution)/shard_map/while/body/eval_jaxpr/ppermute | solution.py:21
  34.8 9.0 %collective-permute-start = (bf16[2,128,256]{1,2,0:T(8,128)(2,1)S(1)}, bf16[2,128,256]{1,2,0:T(8,128)(2,1)S(1)}, u32[]{:S(2)}, u32[]{:S(2)}) collective-permute-start(bf16[2,128,256]{1,2,0:T(8,128)(2,1)S(1)} %get-tuple-element.283), channel_id=1, source_target_pairs={{0,4},{2,6},{4,8},{6,10},{8,12},{10,14},{12,16},{14,18},{16,20},{1... | collective-permute-start | bytes 393224 | tf_op jit(solution)/shard_map/while/body/eval_jaxpr/ppermute | solution.py:21
  43.8 7.8 %collective-permute-start = (bf16[2,128,256]{1,2,0:T(8,128)(2,1)S(1)}, bf16[2,128,256]{1,2,0:T(8,128)(2,1)S(1)}, u32[]{:S(2)}, u32[]{:S(2)}) collective-permute-start(bf16[2,128,256]{1,2,0:T(8,128)(2,1)S(1)} %get-tuple-element.283), channel_id=1, source_target_pairs={{0,4},{2,6},{4,8},{6,10},{8,12},{10,14},{12,16},{14,18},{16,20},{1... | collective-permute-start | bytes 393224 | tf_op jit(solution)/shard_map/while/body/eval_jaxpr/ppermute | solution.py:21
  51.6 9.0 %collective-permute-start = (bf16[2,128,256]{1,2,0:T(8,128)(2,1)S(1)}, bf16[2,128,256]{1,2,0:T(8,128)(2,1)S(1)}, u32[]{:S(2)}, u32[]{:S(2)}) collective-permute-start(bf16[2,128,256]{1,2,0:T(8,128)(2,1)S(1)} %get-tuple-element.283), channel_id=1, source_target_pairs={{0,4},{2,6},{4,8},{6,10},{8,12},{10,14},{12,16},{14,18},{16,20},{1... | collective-permute-start | bytes 393224 | tf_op jit(solution)/shard_map/while/body/eval_jaxpr/ppermute | solution.py:21
  60.6 8.1 %collective-permute-start = (bf16[2,128,256]{1,2,0:T(8,128)(2,1)S(1)}, bf16[2,128,256]{1,2,0:T(8,128)(2,1)S(1)}, u32[]{:S(2)}, u32[]{:S(2)}) collective-permute-start(bf16[2,128,256]{1,2,0:T(8,128)(2,1)S(1)} %get-tuple-element.283), channel_id=1, source_target_pairs={{0,4},{2,6},{4,8},{6,10},{8,12},{10,14},{12,16},{14,18},{16,20},{1... | collective-permute-start | bytes 393224 | tf_op jit(solution)/shard_map/while/body/eval_jaxpr/ppermute | solution.py:21
  68.7 2.5 copy-start.3
  68.7 2.5 copy-start.6
  68.7 2.5 copy-start.7
  188.9 1.9 copy-start.9
  291.3 19.3 %all-to-all-start.3 = ((bf16[4,2,32,2048]{3,2,0,1:T(8,128)(2,1)}), bf16[4,2,32,2048]{3,2,0,1:T(8,128)(2,1)}, u32[]{:S(2)}, u32[]{:S(2)}) async-start(bf16[4,2,32,2048]{3,2,0,1:T(8,128)(2,1)} %copy.80), calls=%async_computation.3 | async-start | bytes 2097152 | tf_op jit(solution)/shard_map/all_to_all | solution.py:146
  295.7 16.2 %copy-start.4 = (bf16[1,128,2048]{2,1,0:T(8,128)(2,1)S(1)}, bf16[1,128,2048]{2,1,0:T(8,128)(2,1)}, u32[]{:S(2)}) copy-start(bf16[1,128,2048]{2,1,0:T(8,128)(2,1)} %param.16) | copy-start | bytes 1572868
  295.7 16.2 %copy-start.8 = (f32[1,128,1]{1,2,0:T(1,128)S(1)}, f32[1,128,1]{1,2,0:T(1,128)}, u32[]{:S(2)}) copy-start(f32[1,128,1]{1,2,0:T(1,128)} %param.19) | copy-start | bytes 1540
  296.9 15.0 %copy-start.5 = (f32[1,128,2048]{2,1,0:T(8,128)S(1)}, f32[1,128,2048]{2,1,0:T(8,128)}, u32[]{:S(2)}) copy-start(f32[1,128,2048]{2,1,0:T(8,128)} %reshape.127) | copy-start | bytes 3145732
where the time goes:
time: 314 us; the launch traced here: 313 us
  blocking collectives  214 us (68%)
  starting transfers between devices  42.1 us (13%)
  waiting for transfers between devices  32.4 us (10%)
  local copies, waits for them, and re-layouts  12.5 us (4%)
  matrix products  7.9 us (3%)
  other arithmetic  4.09 us (1%)
    all_to_all x1, blocking collectives, on_device(): lax.all_to_all(copies, 'ctx', split_axis=0, concat_axis=0, tiled=True)  104 us
    all_to_all x1, blocking collectives, on_device(): lax.all_to_all(partial_value, 'ctx', split_axis=0, concat_axis=0, tiled=T...  97.4 us
    ppermute x7, starting transfers between devices, passed_along(): lax.ppermute(value, axis, [(source, source + steps) for source in range(l...  37.7 us
    ppermute x7, waiting for transfers between devices, passed_along(): lax.ppermute(value, axis, [(source, source + steps) for source in range(l...  18.7 us
    all_to_all x1, waiting for transfers between devices, on_device(): lax.all_to_all(summed.reshape(per_group, exp_count, slot_depth, D), 'exp'...  13.7 us
    all_to_all x1, blocking collectives, on_device(): lax.all_to_all(outgoing, 'exp', split_axis=1, concat_axis=1, tiled=True)  11.9 us
  transfers between devices with their start and end apart: 8, of which 8 were waited for; matrix products, arithmetic and copies ran while one was open for 0% of the time, Pallas kernels for 0%

commit v1 on v0

v1 whole, which is shorter than its diff:
```python
import functools
import math

import jax
import jax.numpy as jnp
from jax import lax
from jax.experimental import pallas as pl
from jax.experimental.pallas import tpu as pltpu
from jax.sharding import PartitionSpec as P

QUERY_HEADS = 16
KEY_VALUE_HEADS = 2
HEAD_SIZE = 128
GROUP_HEADS = QUERY_HEADS // KEY_VALUE_HEADS
KV_WIDTH = KEY_VALUE_HEADS * HEAD_SIZE
NEGATIVE_FILL = -1e30
MESH = pl.DeviceIdType.MESH
NT = (((1,), (1,)), ((), ()))


def layer_kernel(
    ctx_count,
    exp_count,
    slot_depth,
    q_ref,
    k_ref,
    v_ref,
    res_ref,
    gain_ref,
    ids_ref,
    gate_ref,
    wgu_ref,
    wdn_ref,
    out_ref,
    kvbuf,
    peak,
    total,
    acc,
    mid,
    weights,
    outgoing,
    incoming,
    returned,
    local_sem,
    kv_send,
    kv_recv,
    w_send,
    w_recv,
    d_send,
    d_recv,
    r_send,
    r_recv,
):
    tokens, width = q_ref.shape
    quarter = wdn_ref.shape[0]
    ctx = lax.axis_index("ctx")
    exp = lax.axis_index("exp")
    prompt_devs = ctx_count // 2
    prompt = lax.rem(ctx, 2)
    in_prompt = ctx // 2
    per_group = ctx_count // 4
    experts = per_group * exp_count
    place = lax.rem(ctx, 4)
    quad = ctx - place
    own_expert = exp * per_group + ctx // 4
    sibling_place = place + 1 - 2 * lax.rem(place, 2)
    neighbour_place = lax.rem(place + 2, 4)
    sibling = (quad + sibling_place, exp)
    neighbour = (quad + neighbour_place, exp)

    def holder(expert):
        return (lax.rem(expert, per_group) * 4 + place, expert // per_group)

    barrier = pltpu.get_barrier_semaphore()

    def greet(device):
        pl.semaphore_signal(barrier, inc=1, device_id=device, device_id_type=MESH)

    @pl.loop(1, prompt_devs)
    def _(step):
        greet((lax.rem(in_prompt + step, prompt_devs) * 2 + prompt, exp))

    greet(sibling)

    @pl.loop(0, per_group * (exp_count - 1))
    def _(index):
        other = lax.rem(exp + 1 + index // per_group, exp_count)
        greet((lax.rem(index, per_group) * 4 + place, other))

    kvbuf[0, :, :KV_WIDTH] = k_ref[...]
    kvbuf[0, :, KV_WIDTH:] = v_ref[...]
    pl.semaphore_wait(barrier, prompt_devs + per_group * (exp_count - 1))

    def kv_copy(step):
        return pltpu.make_async_remote_copy(
            src_ref=kvbuf.at[0],
            dst_ref=kvbuf.at[step],
            send_sem=kv_send.at[step],
            recv_sem=kv_recv.at[step],
            device_id=((in_prompt + step) * 2 + prompt, exp),
            device_id_type=MESH,
        )

    @pl.loop(1, prompt_devs - in_prompt)
    def _(back):
        kv_copy(prompt_devs - in_prompt - back).start()

    def weight_source(part):
        return wgu_ref.at[part] if part < 2 else wdn_ref

    def weight_rows(part, whose):
        return weights.at[part, pl.ds(pl.multiple_of(whose * quarter, 16), quarter)]

    def weight_copy(part, route):
        whose = neighbour_place if route == 2 else place
        return pltpu.make_async_remote_copy(
            src_ref=weight_rows(part, whose) if route == 2 else weight_source(part),
            dst_ref=weight_rows(part, whose),
            send_sem=w_send.at[route, part],
            recv_sem=w_recv.at[route, part],
            device_id=neighbour if route == 1 else sibling,
            device_id_type=MESH,
        )

    def weight_arrival(part, route):
        whose = (sibling_place, neighbour_place, lax.rem(sibling_place + 2, 4))[route]
        rows = weight_rows(part, whose)
        return pltpu.make_async_remote_copy(
            src_ref=rows,
            dst_ref=rows,
            send_sem=w_send.at[route, part],
            recv_sem=w_recv.at[route, part],
            device_id=sibling,
            device_id_type=MESH,
        )

    def weight_local(part):
        return pltpu.make_async_copy(
            weight_source(part), weight_rows(part, place), local_sem.at[part]
        )

    for part in range(3):
        weight_copy(part, 1).start()
    for part in range(3):
        weight_local(part).start()
        weight_copy(part, 0).start()

    scale = 1.0 / math.sqrt(HEAD_SIZE)

    def attend(slot, first):
        for group in range(KEY_VALUE_HEADS):
            columns = slice(group * HEAD_SIZE, (group + 1) * HEAD_SIZE)
            value_columns = slice(KV_WIDTH + group * HEAD_SIZE, KV_WIDTH + (group + 1) * HEAD_SIZE)
            keys = kvbuf[slot, :, columns]
            values = kvbuf[slot, :, value_columns]
            base = group * GROUP_HEADS
            for head in range(base, base + GROUP_HEADS):
                query = q_ref[:, head * HEAD_SIZE : (head + 1) * HEAD_SIZE]
                scores = lax.dot_general(query, keys, NT, preferred_element_type=jnp.float32)
                scores = scores * scale
                if first:
                    row = lax.broadcasted_iota(jnp.int32, scores.shape, 0)
                    column = lax.broadcasted_iota(jnp.int32, scores.shape, 1)
                    scores = jnp.where(row >= column, scores, NEGATIVE_FILL)
                new_peak = jnp.max(scores, axis=1, keepdims=True)
                if not first:
                    old_peak = peak[head]
                    new_peak = jnp.maximum(old_peak, new_peak)
                expo = jnp.exp(scores - new_peak)
                row_sum = jnp.sum(expo, axis=1, keepdims=True)
                summed = jnp.dot(
                    expo.astype(jnp.bfloat16), values, preferred_element_type=jnp.float32
                )
                if first:
                    total[head] = row_sum
                    acc[head] = summed
                else:
                    factor = jnp.exp(old_peak - new_peak)
                    total[head] = total[head] * factor + row_sum
                    acc[head] = acc[head] * factor + summed
                peak[head] = new_peak

    attend(0, True)

    ids = ids_ref[...]
    lanes = -(-experts // 128) * 128
    onehot = (ids == lax.broadcasted_iota(jnp.int32, (tokens, lanes), 1)).astype(jnp.float32)
    earlier = (
        lax.broadcasted_iota(jnp.int32, (tokens, tokens), 0)
        > lax.broadcasted_iota(jnp.int32, (tokens, tokens), 1)
    ).astype(jnp.float32)
    before = jnp.dot(
        earlier.astype(jnp.bfloat16), onehot.astype(jnp.bfloat16), preferred_element_type=jnp.float32
    )
    rank = jnp.sum(before * onehot, axis=1, keepdims=True)
    slot = ids.astype(jnp.float32) * slot_depth + rank
    slot_lanes = jnp.transpose(jnp.broadcast_to(slot, (tokens, tokens)))[:1, :]

    @pl.loop(1, in_prompt + 1)
    def _(step):
        kv_copy(step).wait_recv()
        attend(step, False)

    for head in range(QUERY_HEADS):
        columns = slice(head * HEAD_SIZE, (head + 1) * HEAD_SIZE)
        attended = acc[head] / total[head]
        mid[:, columns] = (res_ref[:, columns].astype(jnp.float32) + attended).astype(jnp.bfloat16)
    mid_wide = mid[...].astype(jnp.float32)
    inverse = lax.rsqrt(jnp.mean(mid_wide * mid_wide, axis=1, keepdims=True) + 1e-06)
    normed = (mid_wide * inverse * gain_ref[...]).astype(jnp.bfloat16)

    slots = experts * slot_depth
    chunk = min(slots, 256)
    for start in range(0, slots, chunk):
        number = (lax.broadcasted_iota(jnp.int32, (chunk, tokens), 0) + start).astype(jnp.float32)
        pick = (number == slot_lanes).astype(jnp.float32).astype(jnp.bfloat16)
        outgoing[start : start + chunk] = jnp.dot(
            pick, normed, preferred_element_type=jnp.float32
        ).astype(jnp.bfloat16)

    def slot_rows(ref, expert):
        return ref.at[pl.ds(pl.multiple_of(expert * slot_depth, 16), slot_depth)]

    def ahead(step):
        return lax.rem(own_expert + step, experts)

    def behind(step):
        return lax.rem(own_expert + experts - step, experts)

    def dispatch(step):
        return pltpu.make_async_remote_copy(
            src_ref=slot_rows(outgoing, ahead(step)),
            dst_ref=slot_rows(incoming, own_expert),
            send_sem=d_send.at[step],
            recv_sem=d_recv.at[step],
            device_id=holder(ahead(step)),
            device_id_type=MESH,
        )

    def dispatched(step):
        rows = slot_rows(incoming, behind(step))
        return pltpu.make_async_remote_copy(
            src_ref=rows,
            dst_ref=rows,
            send_sem=d_send.at[step],
            recv_sem=d_recv.at[step],
            device_id=holder(behind(step)),
            device_id_type=MESH,
        )

    def give_back(step):
        return pltpu.make_async_remote_copy(
            src_ref=slot_rows(incoming, behind(step)),
            dst_ref=slot_rows(returned, own_expert),
            send_sem=r_send.at[step],
            recv_sem=r_recv.at[step],
            device_id=holder(behind(step)),
            device_id_type=MESH,
        )

    def given_back(step):
        rows = slot_rows(returned, ahead(step))
        return pltpu.make_async_remote_copy(
            src_ref=rows,
            dst_ref=rows,
            send_sem=r_send.at[step],
            recv_sem=r_recv.at[step],
            device_id=holder(ahead(step)),
            device_id_type=MESH,
        )

    @pl.loop(1, experts)
    def _(step):
        dispatch(step).start()

    own_rows = pl.ds(pl.multiple_of(own_expert * slot_depth, 16), slot_depth)
    incoming[own_rows] = outgoing[own_rows]

    for part in range(3):
        weight_arrival(part, 1).wait_recv()
        weight_copy(part, 2).start()

    @pl.loop(1, experts)
    def _(step):
        dispatched(step).wait_recv()

    for part in range(3):
        weight_local(part).wait()
        weight_arrival(part, 0).wait_recv()
        weight_arrival(part, 2).wait_recv()

    def expert_chunk(start):
        rows = incoming[pl.ds(start, chunk)]
        gate = lax.dot_general(rows, weights[0], NT, preferred_element_type=jnp.float32)
        up = lax.dot_general(rows, weights[1], NT, preferred_element_type=jnp.float32)
        hidden = (gate / (1.0 + jnp.exp(-gate)) * up).astype(jnp.bfloat16)
        incoming[pl.ds(start, chunk)] = jnp.dot(
            hidden, weights[2], preferred_element_type=jnp.float32
        ).astype(jnp.bfloat16)

    if slots == chunk:
        expert_chunk(0)
    else:

        @pl.loop(0, slots // chunk)
        def _(index):
            expert_chunk(pl.multiple_of(index * chunk, chunk))

    @pl.loop(1, experts)
    def _(step):
        give_back(step).start()

    returned[own_rows] = incoming[own_rows]

    @pl.loop(1, prompt_devs - in_prompt)
    def _(step):
        kv_copy(step).wait_send()

    for part in range(3):
        for route in range(3):
            weight_copy(part, route).wait_send()

    @pl.loop(1, experts)
    def _(step):
        dispatch(step).wait_send()

    @pl.loop(1, experts)
    def _(step):
        given_back(step).wait_recv()

    number = lax.broadcasted_iota(jnp.int32, (tokens, slots), 1).astype(jnp.float32)
    place_back = (number == slot).astype(jnp.float32).astype(jnp.bfloat16)
    expert_out = jnp.dot(place_back, returned[...], preferred_element_type=jnp.float32)
    out_ref[...] = (mid[...].astype(jnp.float32) + gate_ref[...] * expert_out).astype(jnp.bfloat16)

    @pl.loop(1, experts)
    def _(step):
        give_back(step).wait_send()


def on_device(
    queries,
    rotated_key_rows,
    value_row_array,
    residual,
    norm_gain,
    expert_ids,
    gate_values,
    w_gate_up,
    w_down,
):
    ctx_count = lax.axis_size("ctx")
    exp_count = lax.axis_size("exp")
    tokens, width = queries.shape[1:]
    quarter = w_down.shape[2]
    prompt_devs = ctx_count // 2
    experts = ctx_count // 4 * exp_count
    slot_depth = max(2, 2 * tokens // experts)
    slot_depth = -(-slot_depth // 16) * 16
    slots = experts * slot_depth
    vmem = pl.BlockSpec(memory_space=pltpu.VMEM)
    dma = pltpu.SemaphoreType.DMA
    out = pl.pallas_call(
        functools.partial(layer_kernel, ctx_count, exp_count, slot_depth),
        out_shape=jax.ShapeDtypeStruct((tokens, width), jnp.bfloat16),
        in_specs=[vmem] * 7 + [pl.BlockSpec(memory_space=pl.ANY)] * 2,
        out_specs=vmem,
        scratch_shapes=[
            pltpu.VMEM((prompt_devs, tokens, 2 * KV_WIDTH), jnp.bfloat16),
            pltpu.VMEM((QUERY_HEADS, tokens, 1), jnp.float32),
            pltpu.VMEM((QUERY_HEADS, tokens, 1), jnp.float32),
            pltpu.VMEM((QUERY_HEADS, tokens, HEAD_SIZE), jnp.float32),
            pltpu.VMEM((tokens, width), jnp.bfloat16),
            pltpu.VMEM((3, 4 * quarter, width), jnp.bfloat16),
            pltpu.VMEM((slots, width), jnp.bfloat16),
            pltpu.VMEM((slots, width), jnp.bfloat16),
            pltpu.VMEM((slots, width), jnp.bfloat16),
            dma((3,)),
            dma((prompt_devs,)),
            dma((prompt_devs,)),
            dma((3, 3)),
            dma((3, 3)),
            dma((experts,)),
            dma((experts,)),
            dma((experts,)),
            dma((experts,)),
        ],
        compiler_params=pltpu.CompilerParams(
            collective_id=0, has_side_effects=True, vmem_limit_bytes=58 * 1024 * 1024
        ),
    )(
        queries[0],
        rotated_key_rows[0],
        value_row_array[0],
        residual[0],
        norm_gain[None],
        expert_ids[0],
        gate_values[0],
        w_gate_up[0, 0],
        w_down[0, 0],
    )
    return out[None]


def solution(mesh):
    return jax.shard_map(
        on_device,
        mesh=mesh,
        in_specs=(
            P("exp", "ctx", None),
            P("exp", "ctx", None),
            P("exp", "ctx", None),
            P("exp", "ctx", None),
            P(),
            P("exp", "ctx", None),
            P("exp", "ctx", None),
            P("ctx", "exp", None, None, None),
            P("ctx", "exp", None, None),
        ),
        out_specs=P("exp", "ctx", None),
        check_vma=False,
    )
```

time: 314 us -> 106 us (0.34)
  blocking collectives: 214 us -> 0 us
  Pallas kernels: 0 us -> 102 us
  starting transfers between devices: 42.1 us -> 0 us
  waiting for transfers between devices: 32.4 us -> 0 us
  matrix products: 7.9 us -> 0 us
  local copies, waits for them, and re-layouts: 12.5 us -> 4.65 us
  other arithmetic: 4.09 us -> 0 us
    all_to_all x3 -> x0, blocking collectives: 214 us -> none  [the longest x1 104 us: on_device(): lax.all_to_all(copies, 'ctx', split_axis=0, concat_axis=0, tiled=True)]
    pallas_call x0 -> x1, Pallas kernels: none -> 102 us  [on_device(): pl.pallas_call(functools.partial(layer_kernel, ctx_count, exp_count, slot...]
    ppermute x7 -> x0, starting transfers between devices: 37.7 us -> none  [passed_along(): lax.ppermute(value, axis, [(source, source + steps) for source in range(l...]
    ppermute x7 -> x0, waiting for transfers between devices: 18.7 us -> none  [passed_along(): lax.ppermute(value, axis, [(source, source + steps) for source in range(l...]
    all_to_all x1 -> x0, waiting for transfers between devices: 13.7 us -> none  [on_device(): lax.all_to_all(summed.reshape(per_group, exp_count, slot_depth, D), 'exp'...]
    dot_general x7 -> x0, matrix products: 7.9 us -> none  [the longest x1 1.88 us: on_device(): lax.dot_general(gate_up, flat_rows, (((2,), (1,)), ((), ())), preferred_e...]
    all_to_all x1 -> x0, starting transfers between devices: 4.4 us -> none  [on_device(): lax.all_to_all(summed.reshape(per_group, exp_count, slot_depth, D), 'exp'...]
    unnamed x24 -> x1, local copies, waits for them, and re-layouts: 5.54 us -> 1.88 us
  transfers between devices with their start and end apart: 8 -> 0, of which waited for: 8 -> 0; matrix products, arithmetic and copies ran while one was open for 0% -> 0% of each run, Pallas kernels for 0% -> 0%
where the time goes in v1:
time: 106 us
  Pallas kernels  102 us (96%)
  local copies, waits for them, and re-layouts  4.65 us (4%)
    pallas_call x1, Pallas kernels, on_device(): pl.pallas_call(functools.partial(layer_kernel, ctx_count, exp_count, slot...  102 us

profile of v1, /device:TPU:0, one launch (start us, length us, event | category | flops | bytes accessed | tf_op | source)
XLA Modules:
  0.0 106.2 jit_solution(9969464139272664053)
XLA Ops:
  0.0 1.4 %copy.10.ids_ref = s32[128,1]{1,0:T(8,128)} copy(s32[128,1]{0,1:T(1,128)} %bitcast.18) | data formatting | bytes 1024 | tf_op jit(solution)/shard_map/squeeze | solution.py:397
  1.4 1.4 %copy.11.gate_ref = f32[128,1]{1,0:T(8,128)} copy(f32[128,1]{0,1:T(1,128)} %bitcast.19) | data formatting | bytes 1024 | tf_op jit(solution)/shard_map/squeeze | solution.py:398
  2.8 101.5 %shard_map.91 = bf16[128,2048]{1,0:T(8,128)(2,1)} custom-call(bf16[128,2048]{1,0:T(8,128)(2,1)} %bitcast.13, bf16[128,256]{1,0:T(8,128)(2,1)} %bitcast.15, bf16[128,256]{1,0:T(8,128)(2,1)} %bitcast.16, bf16[128,2048]{1,0:T(8,128)(2,1)} %bitcast.14, f32[1,2048]{1,0:T(1,128)} %bitcast.17, s32[128,1]{1,0:T(8,128)} %copy.10.ids_ref, f32[128,1]{1,0:T(8,128)} %copy.11.gate_ref, ...), custom_call_target="tpu_custom_call" | custom-call | tf_op jit(solution)/shard_map/pallas_call | solution.py:363
  104.3 1.9 %copy.13 = bf16[1,128,2048]{2,1,0:T(8,128)(2,1)} copy(bf16[1,128,2048]{2,1,0:T(8,128)(2,1)} %bitcast.10) | data formatting | bytes 1048576

commit v2 on v1

--- a/solution.py
+++ b/solution.py
@@ -33,6 +33,7 @@
     wdn_ref,
     out_ref,
     kvbuf,
+    stacked,
     peak,
     total,
     acc,
@@ -88,22 +89,53 @@
         greet((lax.rem(index, per_group) * 4 + place, other))
 
     kvbuf[0, :, :KV_WIDTH] = k_ref[...]
-    kvbuf[0, :, KV_WIDTH:] = v_ref[...]
+    for group in range(KEY_VALUE_HEADS):
+        columns = slice(group * HEAD_SIZE, (group + 1) * HEAD_SIZE)
+        value_columns = slice(KV_WIDTH + group * HEAD_SIZE, KV_WIDTH + (group + 1) * HEAD_SIZE)
+        kvbuf[0, :, value_columns] = jnp.transpose(v_ref[:, columns].astype(jnp.float32)).astype(
+            jnp.bfloat16
+        )
     pl.semaphore_wait(barrier, prompt_devs + per_group * (exp_count - 1))
 
-    def kv_copy(step):
+    level = in_prompt // 2
+    side = lax.rem(in_prompt, 2)
+    is_last = level + 1 == prompt_devs // 2
+
+    def kv_swap():
         return pltpu.make_async_remote_copy(
             src_ref=kvbuf.at[0],
-            dst_ref=kvbuf.at[step],
-            send_sem=kv_send.at[step],
-            recv_sem=kv_recv.at[step],
-            device_id=((in_prompt + step) * 2 + prompt, exp),
-            device_id_type=MESH,
-        )
-
-    @pl.loop(1, prompt_devs - in_prompt)
-    def _(back):
-        kv_copy(prompt_devs - in_prompt - back).start()
+            dst_ref=kvbuf.at[1],
+            send_sem=kv_send.at[prompt_devs],
+            recv_sem=kv_recv.at[1],
+            device_id=neighbour,
+            device_id_type=MESH,
+        )
+
+    def kv_up(index):
+        return pltpu.make_async_remote_copy(
+            src_ref=kvbuf.at[index],
+            dst_ref=kvbuf.at[index + 2],
+            send_sem=kv_send.at[index],
+            recv_sem=kv_recv.at[index + 2],
+            device_id=(ctx + 4, exp),
+            device_id_type=MESH,
+        )
+
+    def kv_arrival(index):
+        return pltpu.make_async_remote_copy(
+            src_ref=kvbuf.at[index],
+            dst_ref=kvbuf.at[index],
+            send_sem=kv_send.at[index],
+            recv_sem=kv_recv.at[index],
+            device_id=neighbour,
+            device_id_type=MESH,
+        )
+
+    kv_swap().start()
+
+    @pl.when(jnp.logical_not(is_last))
+    def _():
+        kv_up(0).start()
 
     def weight_source(part):
         return wgu_ref.at[part] if part < 2 else wdn_ref
@@ -145,40 +177,44 @@
         weight_local(part).start()
         weight_copy(part, 0).start()
 
-    scale = 1.0 / math.sqrt(HEAD_SIZE)
+    for head in range(QUERY_HEADS):
+        stacked[head * tokens : (head + 1) * tokens] = q_ref[
+            :, head * HEAD_SIZE : (head + 1) * HEAD_SIZE
+        ]
+    scale = math.log2(math.e) / math.sqrt(HEAD_SIZE)
+    span = GROUP_HEADS * tokens
 
     def attend(slot, first):
         for group in range(KEY_VALUE_HEADS):
+            lanes = slice(group * span, (group + 1) * span)
             columns = slice(group * HEAD_SIZE, (group + 1) * HEAD_SIZE)
             value_columns = slice(KV_WIDTH + group * HEAD_SIZE, KV_WIDTH + (group + 1) * HEAD_SIZE)
-            keys = kvbuf[slot, :, columns]
-            values = kvbuf[slot, :, value_columns]
-            base = group * GROUP_HEADS
-            for head in range(base, base + GROUP_HEADS):
-                query = q_ref[:, head * HEAD_SIZE : (head + 1) * HEAD_SIZE]
-                scores = lax.dot_general(query, keys, NT, preferred_element_type=jnp.float32)
-                scores = scores * scale
-                if first:
-                    row = lax.broadcasted_iota(jnp.int32, scores.shape, 0)
-                    column = lax.broadcasted_iota(jnp.int32, scores.shape, 1)
-                    scores = jnp.where(row >= column, scores, NEGATIVE_FILL)
-                new_peak = jnp.max(scores, axis=1, keepdims=True)
-                if not first:
-                    old_peak = peak[head]
-                    new_peak = jnp.maximum(old_peak, new_peak)
-                expo = jnp.exp(scores - new_peak)
-                row_sum = jnp.sum(expo, axis=1, keepdims=True)
-                summed = jnp.dot(
-                    expo.astype(jnp.bfloat16), values, preferred_element_type=jnp.float32
-                )
-                if first:
-                    total[head] = row_sum
-                    acc[head] = summed
-                else:
-                    factor = jnp.exp(old_peak - new_peak)
-                    total[head] = total[head] * factor + row_sum
-                    acc[head] = acc[head] * factor + summed
-                peak[head] = new_peak
+            scores = lax.dot_general(
+                kvbuf[slot, :, columns], stacked[lanes], NT, preferred_element_type=jnp.float32
+            )
+            if first:
+                key = lax.broadcasted_iota(jnp.int32, scores.shape, 0)
+                query = lax.rem(lax.broadcasted_iota(jnp.int32, scores.shape, 1), tokens)
+                scores = jnp.where(key <= query, scores, NEGATIVE_FILL)
+            new_peak = jnp.max(scores, axis=0, keepdims=True)
+            if not first:
+                old_peak = peak[:, lanes]
+                new_peak = jnp.maximum(old_peak, new_peak)
+            expo = jnp.exp2((scores - new_peak) * scale)
+            row_sum = jnp.sum(expo, axis=0, keepdims=True)
+            summed = jnp.dot(
+                kvbuf[slot, :, value_columns],
+                expo.astype(jnp.bfloat16),
+                preferred_element_type=jnp.float32,
+            )
+            if first:
+                total[:, lanes] = row_sum
+                acc[:, lanes] = summed
+            else:
+                factor = jnp.exp2((old_peak - new_peak) * scale)
+                total[:, lanes] = total[:, lanes] * factor + row_sum
+                acc[:, lanes] = acc[:, lanes] * factor + summed
+            peak[:, lanes] = new_peak
 
     attend(0, True)
 
@@ -196,14 +232,22 @@
     slot = ids.astype(jnp.float32) * slot_depth + rank
     slot_lanes = jnp.transpose(jnp.broadcast_to(slot, (tokens, tokens)))[:1, :]
 
-    @pl.loop(1, in_prompt + 1)
-    def _(step):
-        kv_copy(step).wait_recv()
-        attend(step, False)
+    @pl.loop(1, 2 * level + 2)
+    def _(index):
+        kv_arrival(index).wait_recv()
+
+        @pl.when(jnp.logical_not(is_last))
+        def _():
+            kv_up(index).start()
+
+        @pl.when(jnp.logical_or(index > 1, side == 1))
+        def _():
+            attend(index, False)
 
     for head in range(QUERY_HEADS):
         columns = slice(head * HEAD_SIZE, (head + 1) * HEAD_SIZE)
-        attended = acc[head] / total[head]
+        lanes = slice(head * tokens, (head + 1) * tokens)
+        attended = jnp.transpose(acc[:, lanes] / total[:, lanes])
         mid[:, columns] = (res_ref[:, columns].astype(jnp.float32) + attended).astype(jnp.bfloat16)
     mid_wide = mid[...].astype(jnp.float32)
     inverse = lax.rsqrt(jnp.mean(mid_wide * mid_wide, axis=1, keepdims=True) + 1e-06)
@@ -276,24 +320,36 @@
     own_rows = pl.ds(pl.multiple_of(own_expert * slot_depth, 16), slot_depth)
     incoming[own_rows] = outgoing[own_rows]
 
-    for part in range(3):
+    def hand_on(part):
         weight_arrival(part, 1).wait_recv()
         weight_copy(part, 2).start()
 
+    hand_on(0)
+    hand_on(1)
+
     @pl.loop(1, experts)
     def _(step):
         dispatched(step).wait_recv()
 
-    for part in range(3):
+    def await_weights(part):
+        if part == 2:
+            hand_on(part)
         weight_local(part).wait()
         weight_arrival(part, 0).wait_recv()
         weight_arrival(part, 2).wait_recv()
+
+    await_weights(0)
+    await_weights(1)
+    if slots > chunk:
+        await_weights(2)
 
     def expert_chunk(start):
         rows = incoming[pl.ds(start, chunk)]
         gate = lax.dot_general(rows, weights[0], NT, preferred_element_type=jnp.float32)
         up = lax.dot_general(rows, weights[1], NT, preferred_element_type=jnp.float32)
         hidden = (gate / (1.0 + jnp.exp(-gate)) * up).astype(jnp.bfloat16)
+        if slots == chunk:
+            await_weights(2)
         incoming[pl.ds(start, chunk)] = jnp.dot(
             hidden, weights[2], preferred_element_type=jnp.float32
         ).astype(jnp.bfloat16)
@@ -312,9 +368,13 @@
 
     returned[own_rows] = incoming[own_rows]
 
-    @pl.loop(1, prompt_devs - in_prompt)
-    def _(step):
-        kv_copy(step).wait_send()
+    kv_swap().wait_send()
+
+    @pl.when(jnp.logical_not(is_last))
+    def _():
+        @pl.loop(0, 2 * level + 2)
+        def _(index):
+            kv_up(index).wait_send()
 
     for part in range(3):
         for route in range(3):
@@ -367,16 +427,17 @@
         out_specs=vmem,
         scratch_shapes=[
             pltpu.VMEM((prompt_devs, tokens, 2 * KV_WIDTH), jnp.bfloat16),
-            pltpu.VMEM((QUERY_HEADS, tokens, 1), jnp.float32),
-            pltpu.VMEM((QUERY_HEADS, tokens, 1), jnp.float32),
-            pltpu.VMEM((QUERY_HEADS, tokens, HEAD_SIZE), jnp.float32),
+            pltpu.VMEM((QUERY_HEADS * tokens, HEAD_SIZE), jnp.bfloat16),
+            pltpu.VMEM((1, QUERY_HEADS * tokens), jnp.float32),
+            pltpu.VMEM((1, QUERY_HEADS * tokens), jnp.float32),
+            pltpu.VMEM((HEAD_SIZE, QUERY_HEADS * tokens), jnp.float32),
             pltpu.VMEM((tokens, width), jnp.bfloat16),
             pltpu.VMEM((3, 4 * quarter, width), jnp.bfloat16),
             pltpu.VMEM((slots, width), jnp.bfloat16),
             pltpu.VMEM((slots, width), jnp.bfloat16),
             pltpu.VMEM((slots, width), jnp.bfloat16),
             dma((3,)),
-            dma((prompt_devs,)),
+            dma((prompt_devs + 1,)),
             dma((prompt_devs,)),
             dma((3, 3)),
             dma((3, 3)),

time: 106 us -> 94.8 us (0.89)
  Pallas kernels: 102 us -> 89.8 us
    pallas_call x1, Pallas kernels: 102 us -> 89.8 us  [on_device(): pl.pallas_call(functools.partial(layer_kernel, ctx_count, exp_count, slot...]
where the time goes in v2:
time: 94.8 us; the launch traced here: 94.4 us
  Pallas kernels  89.8 us (95%)
  local copies, waits for them, and re-layouts  4.65 us (5%)
    pallas_call x1, Pallas kernels, on_device(): pl.pallas_call(functools.partial(layer_kernel, ctx_count, exp_count, slot...  89.8 us

profile of v2, /device:TPU:0, one launch (start us, length us, event | category | flops | bytes accessed | tf_op | source)
XLA Modules:
  0.0 94.4 jit_solution(14628977288830081227)
XLA Ops:
  0.0 1.4 %copy.10.ids_ref = s32[128,1]{1,0:T(8,128)} copy(s32[128,1]{0,1:T(1,128)} %bitcast.18) | data formatting | bytes 1024 | tf_op jit(solution)/shard_map/squeeze | solution.py:458
  1.4 1.4 %copy.11.gate_ref = f32[128,1]{1,0:T(8,128)} copy(f32[128,1]{0,1:T(1,128)} %bitcast.19) | data formatting | bytes 1024 | tf_op jit(solution)/shard_map/squeeze | solution.py:459
  2.8 89.8 %shard_map.91 = bf16[128,2048]{1,0:T(8,128)(2,1)} custom-call(bf16[128,2048]{1,0:T(8,128)(2,1)} %bitcast.13, bf16[128,256]{1,0:T(8,128)(2,1)} %bitcast.15, bf16[128,256]{1,0:T(8,128)(2,1)} %bitcast.16, bf16[128,2048]{1,0:T(8,128)(2,1)} %bitcast.14, f32[1,2048]{1,0:T(1,128)} %bitcast.17, s32[128,1]{1,0:T(8,128)} %copy.10.ids_ref, f32[128,1]{1,0:T(8,128)} %copy.11.gate_ref, ...), custom_call_target="tpu_custom_call" | custom-call | tf_op jit(solution)/shard_map/pallas_call | solution.py:423
  92.6 1.9 %copy.13 = bf16[1,128,2048]{2,1,0:T(8,128)(2,1)} copy(bf16[1,128,2048]{2,1,0:T(8,128)(2,1)} %bitcast.10) | data formatting | bytes 1048576

commit v3 on v2

--- a/solution.py
+++ b/solution.py
@@ -218,9 +218,15 @@
 
     attend(0, True)
 
-    ids = ids_ref[...]
+    def down_rows(row):
+        return jnp.transpose(jnp.broadcast_to(row, (tokens, tokens)))[:, :1]
+
+    ids = down_rows(ids_ref[...].astype(jnp.float32))
+    gates = down_rows(gate_ref[...])
     lanes = -(-experts // 128) * 128
-    onehot = (ids == lax.broadcasted_iota(jnp.int32, (tokens, lanes), 1)).astype(jnp.float32)
+    onehot = (
+        ids == lax.broadcasted_iota(jnp.int32, (tokens, lanes), 1).astype(jnp.float32)
+    ).astype(jnp.float32)
     earlier = (
         lax.broadcasted_iota(jnp.int32, (tokens, tokens), 0)
         > lax.broadcasted_iota(jnp.int32, (tokens, tokens), 1)
@@ -229,7 +235,7 @@
         earlier.astype(jnp.bfloat16), onehot.astype(jnp.bfloat16), preferred_element_type=jnp.float32
     )
     rank = jnp.sum(before * onehot, axis=1, keepdims=True)
-    slot = ids.astype(jnp.float32) * slot_depth + rank
+    slot = ids * slot_depth + rank
     slot_lanes = jnp.transpose(jnp.broadcast_to(slot, (tokens, tokens)))[:1, :]
 
     @pl.loop(1, 2 * level + 2)
@@ -391,7 +397,7 @@
     number = lax.broadcasted_iota(jnp.int32, (tokens, slots), 1).astype(jnp.float32)
     place_back = (number == slot).astype(jnp.float32).astype(jnp.bfloat16)
     expert_out = jnp.dot(place_back, returned[...], preferred_element_type=jnp.float32)
-    out_ref[...] = (mid[...].astype(jnp.float32) + gate_ref[...] * expert_out).astype(jnp.bfloat16)
+    out_ref[...] = (mid[...].astype(jnp.float32) + gates * expert_out).astype(jnp.bfloat16)
 
     @pl.loop(1, experts)
     def _(step):
@@ -455,8 +461,8 @@
         value_row_array[0],
         residual[0],
         norm_gain[None],
-        expert_ids[0],
-        gate_values[0],
+        expert_ids.reshape(1, tokens),
+        gate_values.reshape(1, tokens),
         w_gate_up[0, 0],
         w_down[0, 0],
     )

time: 94.8 us -> 92 us (0.970)
  local copies, waits for them, and re-layouts: 4.65 us -> 1.88 us
    squeeze x2 -> x0, local copies, waits for them, and re-layouts: 2.77 us -> none  [the longest x1 1.39 us: on_device(): expert_ids[0]]
where the time goes in v3:
time: 92 us; the launch traced here: 91.7 us
  Pallas kernels  89.8 us (98%)
  local copies, waits for them, and re-layouts  1.88 us (2%)
    pallas_call x1, Pallas kernels, on_device(): pl.pallas_call(functools.partial(layer_kernel, ctx_count, exp_count, slot...  89.8 us
    unnamed x1, local copies, waits for them, and re-layouts  1.88 us

profile of v3, /device:TPU:0, one launch (start us, length us, event | category | flops | bytes accessed | tf_op | source)
XLA Modules:
  0.0 91.7 jit_solution(10562403124345393153)
XLA Ops:
  0.0 89.8 %shard_map.91 = bf16[128,2048]{1,0:T(8,128)(2,1)} custom-call(bf16[128,2048]{1,0:T(8,128)(2,1)} %bitcast.13, bf16[128,256]{1,0:T(8,128)(2,1)} %bitcast.15, bf16[128,256]{1,0:T(8,128)(2,1)} %bitcast.16, bf16[128,2048]{1,0:T(8,128)(2,1)} %bitcast.14, f32[1,2048]{1,0:T(1,128)} %bitcast.17, s32[1,128]{1,0:T(1,128)} %bitcast.18, f32[1,128]{1,0:T(1,128)} %bitcast.19, ...), custom_call_target="tpu_custom_call" | custom-call | tf_op jit(solution)/shard_map/pallas_call | solution.py:429
  89.8 1.9 %copy.11 = bf16[1,128,2048]{2,1,0:T(8,128)(2,1)} copy(bf16[1,128,2048]{2,1,0:T(8,128)(2,1)} %bitcast.10) | data formatting | bytes 1048576
